TPU v7x, 128 devices: a whole 4x4x4 slice. The times are simulated.
128 devices in a mesh: row: 8 (over z_lo, x), col: 16 (over y, z_hi, core).
Axes of the slice: x: 4, y: 4, z: 4 (z_hi: 2, z_lo: 2; z = z_hi * 2 + z_lo), core: 2. Of those that a mesh axis runs over, the one named last changes fastest.
Arguments:
- amplitudes: float32 [2048, 16384], P('col', 'row'), may hold values from -6 to 6
- integrals: float32 [16384, 16384], P('row', 'col'), as said below
- amp_mask: int32 [16, 128], replicated, may hold values 0 or 1
- int_mask: int32 [128, 128], replicated, may hold values 0 or 1
- pairs: int32 [2048, 2], P('row'), may hold values from 0 to 199, as said below
- eps_occ: float32 [200], replicated, may hold values from -2 to -0.3
- eps_vir: float32 [128], replicated, may hold values from 0.3 to 3
Outputs:
- update: float32 [2048, 16384], P('row', 'col')
Inputs may be any that keep to these rules, and one draw needn't show every extreme that they name: `pairs`: rows p and p + 1024 name the same two occupied orbitals in swapped order; the first half holds every pair of 16 distinct orbitals with 64 other distinct orbitals. integrals[c * 128 + d, a * 128 + b] equals integrals[d * 128 + c, b * 128 + a] exactly.
All inputs are finite; a program needn't handle non-finite values.
Results may differ from a plain program's by a relative error of at most 0.000071.
Values sent between devices are 32-bit elements; how exact they have to be, the bound alone decides.
A program may use at most 128 MiB of HBM per device.

v0:
```python
import jax
import jax.numpy as jnp
from jax import lax
from jax.sharding import PartitionSpec as P

TILE = 128


def partner_2(x, axis, apart):
    return lax.ppermute(x, axis, [(i, i ^ 1 << apart) for i in range(lax.axis_size(axis))])


def on_device(amplitudes, integrals, amp_mask, int_mask, pairs, eps_occ, eps_vir):
    n_row = lax.axis_size("row")
    n_col = lax.axis_size("col")
    row_index = lax.axis_index("row")
    col_index = lax.axis_index("col")
    width = eps_vir.shape[0]
    c_local = width // n_row
    a_local = width // n_col
    amp_rows = amplitudes.shape[0]
    tile_count = amp_mask.shape[0]
    global_rows = col_index * amp_rows + jnp.arange(amp_rows, dtype=jnp.int32)
    picked = (
        global_rows[:, None] // TILE == jnp.arange(tile_count, dtype=jnp.int32)[None, :]
    ).astype(jnp.float32)
    row_mask = jnp.dot(
        picked,
        amp_mask.astype(jnp.float32),
        precision=lax.Precision.HIGHEST,
        preferred_element_type=jnp.float32,
    )
    row_mask = lax.dynamic_slice_in_dim(row_mask, row_index * c_local, c_local, 1)
    masked = amplitudes.reshape(amp_rows, c_local, width) * row_mask[:, :, None]
    coupling = int_mask.astype(jnp.float32)
    block_mask = lax.dynamic_slice(
        coupling, (row_index * c_local, col_index * a_local), (c_local, a_local)
    )
    weighted = (
        integrals.reshape(c_local, width, a_local, width)
        * block_mask[:, None, :, None]
        * coupling[None, :, None, :]
    )
    weighted = weighted.reshape(c_local * width, a_local * width)
    flat = masked.reshape(amp_rows, c_local * width)
    gathered = lax.all_gather(flat, "col", axis=0, tiled=True)
    result = lax.psum_scatter(
        jnp.dot(
            gathered, weighted, precision=lax.Precision.HIGHEST, preferred_element_type=jnp.float32
        ),
        "row",
        scatter_dimension=0,
        tiled=True,
    )
    out_rows = result.shape[0]
    partner = partner_2(result, "row", n_row.bit_length() - 2)
    turned = lax.all_to_all(
        partner.reshape(out_rows, a_local, width), "col", split_axis=2, concat_axis=1, tiled=True
    )
    result = result + jnp.swapaxes(turned, 1, 2).reshape(out_rows, a_local * width)
    occ_ids = jnp.arange(eps_occ.shape[0], dtype=jnp.int32)
    first = jnp.sum(
        jnp.where(pairs[:, 0:1] == occ_ids[None, :], eps_occ[None, :], jnp.float32(0.0)), axis=1
    )
    second = jnp.sum(
        jnp.where(pairs[:, 1:2] == occ_ids[None, :], eps_occ[None, :], jnp.float32(0.0)), axis=1
    )
    occ_energy = first + second
    vir_local = lax.dynamic_slice_in_dim(eps_vir, col_index * a_local, a_local, 0)
    denom = (vir_local[:, None] + eps_vir[None, :])[None, :, :] - occ_energy[:, None, None]
    return (result.reshape(out_rows, a_local, width) / denom).reshape(out_rows, a_local * width)


def solution(mesh):
    return jax.shard_map(
        on_device,
        mesh=mesh,
        in_specs=(P("col", "row"), P("row", "col"), P(), P(), P("row", None), P(), P()),
        out_specs=P("row", "col"),
        check_vma=False,
    )
```

profile of v0, /device:TPU:1, one launch (start us, length us, event | category | flops | bytes accessed | tf_op | source)
XLA Modules:
  0.0 338.6 jit_solution(5816041840554046056)
XLA Ops:
  6.5 0.0 all-gather.2.cloned.1.call-start
  6.5 1.0 fusion.4
  7.5 0.1 copy.19
  7.6 0.3 mul.46
  8.0 2.6 bitcast_multiply_fusion.4
  10.6 0.0 all-gather.2.cloned.1.call-update
  10.7 0.0 reduce-scatter.2.cloned.1.call-start
  10.7 0.8 convert_element_type.8
  11.6 0.1 dynamic_slice.10
  11.6 113.2 %all-gather.2.cloned.1.call-done = f32[2048,2048]{1,0:T(8,128)} async-done(((f32[128,2048]{1,0:T(8,128)}), f32[2048,2048]{1,0:T(8,128)}) %all-gather.2.cloned.1.call-update) | async-done | bytes 16777232 | tf_op jit(solution)/shard_map/all_gather | solution.py:46
  124.8 0.6 mul.50
  125.4 0.8 mul.53
  126.2 62.0 %fusion = f32[2048,1024]{1,0:T(8,128)} fusion(f32[2048,2048]{1,0:T(8,128)} %all-gather.2.cloned.1.call-done, f32[256,8,8,128]{3,2,1,0:T(8,128)S(1)} %bitcast.40, f32[2048,1024]{1,0:T(8,128)} %param.8, f32[256,8,8,128]{3,2,1,0:T(8,128)S(1)} %bitcast.39), kind=kOutput, calls=%fused_computation.1 | convolution fusion | flops 51543801856 | bytes 50331648 | tf_op jit(solution)/shard_map/dot_general | solution.py:48
  188.2 0.0 copy-start.3
  188.2 0.0 copy-start.1
  188.2 0.0 copy-start.2
  188.2 0.0 reduce-scatter.2.cloned.1.call-update
  188.2 90.0 %reduce-scatter.2.cloned.1.call-done = f32[256,1024]{1,0:T(8,128)} async-done(((f32[2048,1024]{1,0:T(8,128)}), f32[256,1024]{1,0:T(8,128)}) %reduce-scatter.2.cloned.1.call-update) | async-done | bytes 1048592 | tf_op jit(solution)/shard_map/reduce_scatter | solution.py:47
  278.2 0.0 copy-start
  278.2 0.2 collective-permute-start
  278.4 24.1 %collective-permute-done = f32[256,1024]{1,0:T(8,128)S(1)} collective-permute-done((f32[256,1024]{1,0:T(8,128)}, f32[256,1024]{1,0:T(8,128)S(1)}, u32[]{:S(2)}, u32[]{:S(2)}) %collective-permute-start) | collective-permute-done | bytes 1048608 | tf_op jit(solution)/shard_map/ppermute | solution.py:10
  302.5 0.2 copy.28
  302.7 1.5 copy.20
  304.2 8.1 %all-to-all-start = ((f32[256,8,128]{0,1,2:T(8,128)}), f32[256,8,128]{0,1,2:T(8,128)S(1)}, u32[]{:S(2)}, u32[]{:S(2)}) async-start(f32[256,8,128]{0,1,2:T(8,128)} %copy.20), calls=%async_computation.1 | async-start | bytes 2097152 | tf_op jit(solution)/shard_map/all_to_all | solution.py:57
  312.3 0.0 copy-done.3
  312.3 0.1 dynamic_slice.11
  312.4 0.0 copy-done.1
  312.4 0.0 copy-done.2
  312.4 0.1 select_reduce_fusion
  312.5 0.1 add.62
  312.6 16.9 %all-to-all-done = f32[256,8,128]{0,1,2:T(8,128)S(1)} async-done(((f32[256,8,128]{0,1,2:T(8,128)}), f32[256,8,128]{0,1,2:T(8,128)S(1)}, u32[]{:S(2)}, u32[]{:S(2)}) %all-to-all-start) | async-done | bytes 1048608 | tf_op jit(solution)/shard_map/all_to_all | solution.py:57
  329.5 0.3 copy.22
  329.9 0.6 copy.23
  330.5 0.0 copy-done
  330.5 1.3 fusion.3
  (5 shorter events, 0.0 us)
Async XLA Ops:
  6.5 118.2 %all-gather.2.cloned.1.call-start = ((), (), s32[]{:S(2)}) async-start(), calls=%async_computation.2 | async-start | bytes 17825792 | tf_op jit(solution)/shard_map/all_gather | solution.py:46
  10.7 267.6 %reduce-scatter.2.cloned.1.call-start = ((), (), s32[]{:S(2)}) async-start(), calls=%async_computation.3 | async-start | bytes 9437184 | tf_op jit(solution)/shard_map/reduce_scatter | solution.py:47
  188.2 124.1 %copy-start.3 = (f32[128]{0:T(128)S(1)}, f32[128]{0:T(128)}, u32[]{:S(2)}) copy-start(f32[128]{0:T(128)} %param.13) | copy-start | bytes 1540
  188.2 124.2 %copy-start.1 = (s32[256,2]{0,1:T(2,128)S(1)}, s32[256,2]{0,1:T(2,128)}, u32[]{:S(2)}) copy-start(s32[256,2]{0,1:T(2,128)} %param.11) | copy-start | bytes 6148
  188.2 124.2 %copy-start.2 = (f32[200]{0:T(256)S(1)}, f32[200]{0:T(256)}, u32[]{:S(2)}) copy-start(f32[200]{0:T(256)} %param.12) | copy-start | bytes 2404
  278.2 52.3 %copy-start = (f32[256,1024]{1,0:T(8,128)S(1)}, f32[256,1024]{1,0:T(8,128)}, u32[]{:S(2)}) copy-start(f32[256,1024]{1,0:T(8,128)} %reduce-scatter.2.cloned.1.call-done) | copy-start | bytes 3145732
  278.2 24.3 %collective-permute-start = (f32[256,1024]{1,0:T(8,128)}, f32[256,1024]{1,0:T(8,128)S(1)}, u32[]{:S(2)}, u32[]{:S(2)}) collective-permute-start(f32[256,1024]{1,0:T(8,128)} %reduce-scatter.2.cloned.1.call-done), channel_id=1, source_target_pairs={{0,64},{16,80},{32,96},{48,112},{64,0},{80,16},{96,32},{112,48},{1... | collective-permute-start | bytes 3145736 | tf_op jit(solution)/shard_map/ppermute | solution.py:10
  304.2 25.3 %all-to-all-start = ((f32[256,8,128]{0,1,2:T(8,128)}), f32[256,8,128]{0,1,2:T(8,128)S(1)}, u32[]{:S(2)}, u32[]{:S(2)}) async-start(f32[256,8,128]{0,1,2:T(8,128)} %copy.20), calls=%async_computation.1 | async-start | bytes 2097152 | tf_op jit(solution)/shard_map/all_to_all | solution.py:57
Sparse Core Ops, SparseCore 0:
  10.8 113.9 all-gather.1
  188.3 89.8 reduce-scatter.1
where the time goes:
time: 339 us
  waiting for transfers between devices  244 us (72%)
  matrix products  62.9 us (19%)
  between operations  13.5 us (4%)
  starting transfers between devices  8.37 us (2%)
  other arithmetic  4.9 us (1%)
  local copies, waits for them, and re-layouts  4.72 us (1%)
    all_gather x1, waiting for transfers between devices, on_device(): gathered = lax.all_gather(flat, 'col', axis=0, tiled=True)  113 us
    reduce_scatter x1, waiting for transfers between devices, on_device(): lax.psum_scatter(jnp.dot(gathered, weighted, precision=lax.Precision.HIGH...  90 us
    dot_general x1, matrix products, on_device(): jnp.dot(gathered, weighted, precision=lax.Precision.HIGHEST, preferred_el...  62 us
    ppermute x1, waiting for transfers between devices, partner_2(): lax.ppermute(x, axis, [(i, i ^ 1 << apart) for i in range(lax.axis_size(a...  24.1 us
    all_to_all x1, waiting for transfers between devices, on_device(): lax.all_to_all(partner.reshape(out_rows, a_local, width), 'col', split_ax...  16.9 us
    all_to_all x1, starting transfers between devices, on_device(): lax.all_to_all(partner.reshape(out_rows, a_local, width), 'col', split_ax...  8.12 us
  transfers between devices with their start and end apart: 4, of which 4 were waited for; matrix products, arithmetic and copies ran while one was open for 0% of the time, Pallas kernels for 0%

commit v1 on v0

v1 whole, which is shorter than its diff:
```python
import functools

import jax
import jax.numpy as jnp
from jax import lax
from jax.experimental import pallas as pl
from jax.experimental.pallas import tpu as pltpu
from jax.sharding import PartitionSpec as P

MESH = pl.DeviceIdType.MESH
ROUNDS = 4
ROWS = 64 // ROUNDS
HALF = ROWS // 2
F32 = jnp.float32
BF16 = jnp.bfloat16


def swap_bits(tiles, tile_bit, lane_bit):
    step = 1 << lane_bit
    lane = lax.broadcasted_iota(jnp.int32, tiles[0].shape, len(tiles[0].shape) - 1)
    upper = (lane & step) != 0
    result = list(tiles)
    for low in range(len(tiles)):
        if low >> tile_bit & 1:
            continue
        high = low | 1 << tile_bit
        a, b = tiles[low], tiles[high]
        result[low] = jnp.where(upper, pltpu.roll(b, step, 1), a)
        result[high] = jnp.where(upper, b, pltpu.roll(a, 128 - step, 1))
    return result


def split(value):
    hi = value.astype(BF16)
    return hi, (value - hi.astype(F32)).astype(BF16)


def kernel(
    t_hbm, v_hbm, am_s, im_s, im_v, pairs_v, eocc_v, evir_v, evir_s,
    out,
    tbuf, vbuf, vhi, vlo, pre_s, pre_r, slab, shi, slo, part, xr, zb, zr, post_s, post_r, occ, imf,
    load_sem, pre_ss, pre_rs, g_ss, g_rs, c_ss, c_rs, x_ss, x_rs, z_ss, z_rs, o_ss, o_rs,
):
    row = lax.axis_index("row")
    col = lax.axis_index("col")
    zlo, x = row // 4, lax.rem(row, 4)
    y, zhi, core = col // 4, lax.rem(col // 2, 2), lax.rem(col, 2)
    chip = col // 2
    row_z = lax.rem(row + 4, 8)
    col_far = lax.rem(col + 8, 16)
    up = lax.rem(y + 1, 4)
    down = lax.rem(y + 3, 4)
    opposite = lax.rem(y + 2, 4)
    flip = 1 - zhi

    def col_of(yy, zz):
        return yy * 4 + zz * 2 + core

    dev_up = (row, col_of(up, zhi))
    dev_down = (row, col_of(down, zhi))
    dev_z = (row, col_of(y, flip))
    dev_core = (row, chip * 2 + 1 - core)
    dev_zlo = (row_z, col)
    own_off = 64 * (y // 2)
    send_off = 64 - own_off

    barrier = pltpu.get_barrier_semaphore()
    peers = [(r, col_far) for r in range(8)]
    peers += [dev_up, dev_down, dev_z, dev_core]
    peers += [(zlo * 4 + lax.rem(x + dx, 4), col) for dx in (1, 2, 3)]
    peers += [(row_z, lax.rem(col + j, 16)) for j in range(16) if j != 8]
    for peer in peers:
        pl.semaphore_signal(barrier, inc=1, device_id=peer, device_id_type=MESH)

    t_load = pltpu.make_async_copy(t_hbm, tbuf, load_sem.at[16])
    t_load.start()

    def v_load(block):
        rows = pl.ds(block * 128, 128)
        return pltpu.make_async_copy(v_hbm.at[rows], vbuf.at[rows], load_sem.at[block])

    for block in range(16):
        v_load(block).start()

    def remote(src, dst, send_sem, recv_sem, device):
        return pltpu.make_async_remote_copy(
            src_ref=src, dst_ref=dst, send_sem=send_sem, recv_sem=recv_sem,
            device_id=device, device_id_type=MESH,
        )

    def drain(ref, sem):
        pltpu.make_async_copy(ref, ref, sem).wait()

    imf[...] = im_v[...].astype(F32)

    ids = lax.broadcasted_iota(jnp.int32, (256, 200), 1)
    first = jnp.sum(jnp.where(pairs_v[:, 0:1] == ids, eocc_v[...], 0.0), axis=1, keepdims=True)
    second = jnp.sum(jnp.where(pairs_v[:, 1:2] == ids, eocc_v[...], 0.0), axis=1, keepdims=True)
    occ[...] = jnp.broadcast_to(first + second, (256, 128))

    t_load.wait()

    def masked_tile(offset, q, j):
        rows = pl.ds(pl.multiple_of(offset + q * ROWS, 8), ROWS)
        return tbuf[rows, j * 128 : (j + 1) * 128] * am_s[col, row * 16 + j].astype(F32)

    def pre_shuffle(q):
        tiles = [masked_tile(send_off, q, j) for j in range(16)]
        for bit in range(4):
            tiles = swap_bits(tiles, bit, bit)
        for bit in range(3):
            tiles = swap_bits(tiles, bit, bit + 4)
        for j in range(16):
            pre_s[q, j % 8, j // 8] = tiles[j]

    def pre_send(q):
        for r in range(8):
            remote(
                pre_s.at[q, r], pre_r.at[q, row], pre_ss.at[q], pre_rs.at[q], (r, col_far)
            ).start()

    pre_shuffle(0)
    pl.semaphore_wait(barrier, len(peers))
    pre_send(0)
    pre_shuffle(1)
    pre_send(1)
    for q in range(2, ROUNDS):
        pre_shuffle(q)

    def convert(block, _):
        v_load(block).wait()
        rows = pl.ds(pl.multiple_of(block * 128, 128), 128)
        for al in range(8):
            lanes = slice(al * 128, (al + 1) * 128)
            weight = im_s[row * 16 + block, col * 8 + al].astype(F32)
            hi, lo = split(vbuf[rows, lanes] * imf[...] * weight)
            vhi[rows, lanes] = hi
            vlo[rows, lanes] = lo
        return 0

    def slot(q, yy, zz, rows=None):
        ref = slab.at[q, core, yy * 2 + zz]
        return ref if rows is None else ref.at[rows]

    LOWER, UPPER = pl.ds(0, HALF), pl.ds(HALF, HALF)

    def push(q, kind, yy, zz, device, rows=None):
        ref = slot(q, yy, zz, rows)
        remote(ref, ref, g_ss.at[q], g_rs.at[q, kind], device).start()

    def arrived(q, kind, yy, zz, rows=None):
        drain(slot(q, yy, zz, rows), g_rs.at[q, kind])

    def to_core(q, yy, zz):
        ref = slot(q, yy, zz)
        remote(ref, ref, c_ss.at[q], c_rs.at[q], dev_core).start()

    def g1(q):
        drain(pre_r.at[q], pre_rs.at[q])
        tiles = [pre_r[q, j % 8, j // 8] for j in range(16)]
        for bit in range(3):
            tiles = swap_bits(tiles, bit, bit + 4)
        for j in range(16):
            slab[q, core, chip, :, j * 128 : (j + 1) * 128] = masked_tile(own_off, q, j) + tiles[j]
        push(q, 0, y, zhi, dev_z)
        push(q, 1, y, zhi, dev_up)
        push(q, 2, y, zhi, dev_down)
        to_core(q, y, zhi)

    def g2(q):
        arrived(q, 1, down, zhi)
        push(q, 3, down, zhi, dev_up, LOWER)
        to_core(q, down, zhi)
        arrived(q, 2, up, zhi)
        push(q, 4, up, zhi, dev_down, UPPER)
        to_core(q, up, zhi)
        arrived(q, 0, y, flip)
        push(q, 5, y, flip, dev_up)
        push(q, 6, y, flip, dev_down)
        to_core(q, y, flip)

    def g3(q):
        arrived(q, 3, opposite, zhi, LOWER)
        arrived(q, 4, opposite, zhi, UPPER)
        to_core(q, opposite, zhi)
        arrived(q, 5, down, flip)
        push(q, 7, down, flip, dev_up, LOWER)
        to_core(q, down, flip)
        arrived(q, 6, up, flip)
        push(q, 8, up, flip, dev_down, UPPER)
        to_core(q, up, flip)

    def g4(q):
        arrived(q, 7, opposite, flip, LOWER)
        arrived(q, 8, opposite, flip, UPPER)
        to_core(q, opposite, flip)

    def mm(q):
        drain(slab.at[q, 0], c_rs.at[q])
        for k in range(2):
            for c in range(8):
                rows = slice((k * 8 + c) * ROWS, (k * 8 + c + 1) * ROWS)
                hi, lo = split(slab[q, k, c])
                shi[rows, :] = hi
                slo[rows, :] = lo

        def tile(n, _):
            lanes = pl.ds(pl.multiple_of(n * 256, 256), 256)
            dot = functools.partial(jnp.dot, preferred_element_type=F32)
            acc = dot(shi[...], vhi[:, lanes])
            acc += dot(slo[...], vhi[:, lanes])
            acc += dot(shi[...], vlo[:, lanes])
            part[q, :, :, :, :, lanes] = acc.reshape(2, 2, 4, ROWS, 256)
            return 0

        lax.fori_loop(0, 4, tile, 0)
        for dx in (1, 2, 3):
            there = lax.rem(x + dx, 4)
            remote(
                part.at[q, :, :, there], xr.at[q, dx - 1], x_ss.at[q], x_rs.at[q],
                (zlo * 4 + there, col),
            ).start()

    def rx(q):
        drain(xr.at[q], x_rs.at[q])
        for side in (1, 0):
            z = lax.rem(zlo + side, 2)
            for k in range(2):
                zb[q, side, k] = (
                    (part[q, k, z, x] + xr[q, 0, k, z]) + (xr[q, 1, k, z] + xr[q, 2, k, z])
                )
            if side:
                remote(zb.at[q, 1], zr.at[q], z_ss.at[q], z_rs.at[q], dev_zlo).start()

    def out_rows(k, z, q):
        return pl.ds(pl.multiple_of(k * 128 + 64 * z + q * ROWS, 8), ROWS)

    def rz(q):
        drain(zr.at[q], z_rs.at[q])
        tiles = []
        for k in range(2):
            rows = out_rows(k, zlo, q)
            for al in range(8):
                lanes = slice(al * 128, (al + 1) * 128)
                denom = (evir_s[0, col * 8 + al] + evir_v[...]) - occ[rows, :]
                value = (zb[q, 0, k, :, lanes] + zr[q, k, :, lanes]) / denom
                out[rows, lanes] = value
                tiles.append(value)
        for bit in range(3):
            tiles = swap_bits(tiles, bit, bit)
        for bit in range(3):
            tiles = swap_bits(tiles, bit, bit + 3)
        tiles = swap_bits(tiles, 3, 6)
        for c in range(16):
            post_s[q, c] = tiles[c]
        for c in range(16):
            remote(
                post_s.at[q, c], post_r.at[q, col], o_ss.at[q], o_rs.at[q], (row_z, c)
            ).start()

    def fin(q):
        drain(post_r.at[q], o_rs.at[q])
        tiles = [post_r[q, c] for c in range(16)]
        for bit in range(3):
            tiles = swap_bits(tiles, bit, bit + 3)
        tiles = swap_bits(tiles, 3, 6)
        for k in range(2):
            for bl in range(8):
                out[out_rows(k, 1 - zlo, q), bl * 128 : (bl + 1) * 128] = tiles[k * 8 + bl]

    def when(stage, q):
        if 0 <= q < ROUNDS:
            stage(q)

    for i in range(ROUNDS + 3):
        when(g1, i)
        if i + 2 < ROUNDS:
            pre_send(i + 2)
        when(rz, i - 3)
        if i == 0:
            lax.fori_loop(0, 16, convert, 0)
        when(g4, i - 1)
        when(g2, i)
        when(mm, i - 1)
        when(rx, i - 2)
        when(g3, i)
        when(fin, i - 3)

    for q in range(ROUNDS):
        drain(pre_s.at[q], pre_ss.at[q])
        drain(slab.at[q, 0, pl.ds(0, 7)], g_ss.at[q])
        drain(slab.at[q, 0], c_ss.at[q])
        drain(xr.at[q], x_ss.at[q])
        drain(zr.at[q], z_ss.at[q])
        drain(post_s.at[q], o_ss.at[q])


def on_device(amplitudes, integrals, amp_mask, int_mask, pairs, eps_occ, eps_vir):
    vmem = pl.BlockSpec(memory_space=pltpu.VMEM)
    smem = pl.BlockSpec(memory_space=pltpu.SMEM)
    hbm = pl.BlockSpec(memory_space=pl.ANY)
    dma = pltpu.SemaphoreType.DMA
    n = ROUNDS
    eps_vir = eps_vir.reshape(1, 128)
    return pl.pallas_call(
        kernel,
        out_shape=jax.ShapeDtypeStruct((256, 1024), F32),
        in_specs=[hbm, hbm, smem, smem, vmem, vmem, vmem, vmem, smem],
        out_specs=vmem,
        scratch_shapes=[
            pltpu.VMEM((128, 2048), F32),
            pltpu.VMEM((2048, 1024), F32),
            pltpu.VMEM((2048, 1024), BF16),
            pltpu.VMEM((2048, 1024), BF16),
            pltpu.VMEM((n, 8, 2, ROWS, 128), F32),
            pltpu.VMEM((n, 8, 2, ROWS, 128), F32),
            pltpu.VMEM((n, 2, 8, ROWS, 2048), F32),
            pltpu.VMEM((16 * ROWS, 2048), BF16),
            pltpu.VMEM((16 * ROWS, 2048), BF16),
            pltpu.VMEM((n, 2, 2, 4, ROWS, 1024), F32),
            pltpu.VMEM((n, 3, 2, 2, ROWS, 1024), F32),
            pltpu.VMEM((n, 2, 2, ROWS, 1024), F32),
            pltpu.VMEM((n, 2, ROWS, 1024), F32),
            pltpu.VMEM((n, 16, ROWS, 128), F32),
            pltpu.VMEM((n, 16, ROWS, 128), F32),
            pltpu.VMEM((256, 128), F32),
            pltpu.VMEM((128, 128), F32),
            dma((17,)),
            dma((n,)), dma((n,)),
            dma((n,)), dma((n, 9)),
            dma((n,)), dma((n,)),
            dma((n,)), dma((n,)),
            dma((n,)), dma((n,)),
            dma((n,)), dma((n,)),
        ],
        compiler_params=pltpu.CompilerParams(
            collective_id=0, has_side_effects=True, vmem_limit_bytes=60 * 2**20
        ),
        cost_estimate=pl.CostEstimate(
            flops=3 * 2 * 1024 * 2048 * 1024, bytes_accessed=10 * 2**20, transcendentals=0
        ),
        name="ladder",
    )(
        amplitudes, integrals, amp_mask, int_mask, int_mask, pairs,
        eps_occ.reshape(1, 200), eps_vir, eps_vir,
    )


def solution(mesh):
    return jax.shard_map(
        on_device,
        mesh=mesh,
        in_specs=(P("col", "row"), P("row", "col"), P(), P(), P("row", None), P(), P()),
        out_specs=P("row", "col"),
        check_vma=False,
    )
```

time: 339 us -> 113 us (0.33)
  waiting for transfers between devices: 244 us -> 0 us
  Pallas kernels: 0 us -> 109 us
  matrix products: 62.9 us -> 0 us
  between operations: 13.5 us -> 0.01 us
  starting transfers between devices: 8.37 us -> 0 us
  other arithmetic: 4.9 us -> 0 us
    all_gather x1 -> x0, waiting for transfers between devices: 113 us -> none  [on_device(): gathered = lax.all_gather(flat, 'col', axis=0, tiled=True)]
    pallas_call x0 -> x1, Pallas kernels: none -> 109 us  [on_device(): pl.pallas_call(kernel, out_shape=jax.ShapeDtypeStruct((256, 1024), F32),...]
    reduce_scatter x1 -> x0, waiting for transfers between devices: 90 us -> none  [on_device(): lax.psum_scatter(jnp.dot(gathered, weighted, precision=lax.Precision.HIGH...]
    dot_general x2 -> x0, matrix products: 62.9 us -> none  [the longest x1 62 us: on_device(): jnp.dot(gathered, weighted, precision=lax.Precision.HIGHEST, preferred_el...]
    ppermute x1 -> x0, waiting for transfers between devices: 24.1 us -> none  [partner_2(): lax.ppermute(x, axis, [(i, i ^ 1 << apart) for i in range(lax.axis_size(a...]
    all_to_all x1 -> x0, waiting for transfers between devices: 16.9 us -> none  [on_device(): lax.all_to_all(partner.reshape(out_rows, a_local, width), 'col', split_ax...]
    all_to_all x1 -> x0, starting transfers between devices: 8.12 us -> none  [on_device(): lax.all_to_all(partner.reshape(out_rows, a_local, width), 'col', split_ax...]
    unnamed x9 -> x2, local copies, waits for them, and re-layouts: 0.21 us -> 3.78 us
  transfers between devices with their start and end apart: 4 -> 0, of which waited for: 4 -> 0; matrix products, arithmetic and copies ran while one was open for 0% -> 0% of each run, Pallas kernels for 0% -> 0%
where the time goes in v1:
time: 113 us; the launch traced here: 112 us
  Pallas kernels  109 us (96%)
  local copies, waits for them, and re-layouts  3.78 us (3%)
    pallas_call x1, Pallas kernels, on_device(): pl.pallas_call(kernel, out_shape=jax.ShapeDtypeStruct((256, 1024), F32),...  109 us
    unnamed x2, local copies, waits for them, and re-layouts  3.78 us

profile of v1, /device:TPU:1, one launch (start us, length us, event | category | flops | bytes accessed | tf_op | source)
XLA Modules:
  0.0 112.4 jit_solution(3218049199410175917)
XLA Ops:
  0.0 1.5 %copy.8.pairs_v = s32[256,2]{1,0:T(8,128)} copy(s32[256,2]{0,1:T(2,128)} %param.11) | data formatting | bytes 4096 | tf_op args[4]
  1.5 108.6 %ladder.1 = f32[256,1024]{1,0:T(8,128)} custom-call(f32[128,2048]{1,0:T(8,128)} %t_hbm.1, f32[2048,1024]{1,0:T(8,128)} %v_hbm.1, s32[16,128]{1,0:T(8,128)} %am_s.1, s32[128,128]{1,0:T(8,128)} %im_v.1, s32[128,128]{1,0:T(8,128)} %im_v.1, s32[256,2]{1,0:T(8,128)} %copy.8.pairs_v, f32[1,200]{1,0:T(1,128)} %bitcast.2, f32[1,128]{1,0:T(1,128)} %bitcast.3, ...), custom_call_target="tpu_custom_call" | custom-call | flops 12884901888 | bytes 10485760 | tf_op jit(solution)/shard_map/ladder/pallas_call | solution.py:305
  110.1 2.3 %copy.10 = f32[256,1024]{1,0:T(8,128)} copy(f32[256,1024]{1,0:T(8,128)} %ladder.1) | data formatting | bytes 2097152

commit v2 on v1

--- a/solution.py
+++ b/solution.py
@@ -8,11 +8,27 @@
 from jax.sharding import PartitionSpec as P
 
 MESH = pl.DeviceIdType.MESH
-ROUNDS = 4
+ROUNDS = 8
 ROWS = 64 // ROUNDS
-HALF = ROWS // 2
 F32 = jnp.float32
 BF16 = jnp.bfloat16
+Y_FIRST = frozenset((1, 3, 5,))
+ORDER = (
+    ("P", 0), ("P", 1), ("P", 2), ("P", 3), ("C", 0), ("P", 4), ("C", 1), ("G1", 0), ("G1", 1),
+    ("G1", 2), ("G2a", 0), ("G2b", 0), ("G2a", 1), ("G2b", 1), ("G1", 3), ("G2a", 2), ("G3a", 0),
+    ("G3b", 0), ("P", 5), ("C", 2), ("G2b", 2), ("G3a", 1), ("G1", 4), ("C", 3), ("G3a", 2),
+    ("P", 6), ("G4", 0), ("G2a", 3), ("G3b", 1), ("MA", 0), ("G4", 1), ("G2b", 3), ("G3b", 2),
+    ("MB", 0), ("G1", 5), ("P", 7), ("MA", 1), ("G2a", 4), ("G4", 2), ("G3a", 3), ("MB", 1),
+    ("G2b", 4), ("G3b", 3), ("X1", 0), ("G2a", 5), ("G1", 6), ("MA", 2), ("MB", 2), ("G4", 3),
+    ("G3a", 4), ("G3b", 4), ("X1", 1), ("G2b", 5), ("G1", 7), ("G3a", 5), ("MA", 3), ("G2a", 6),
+    ("G4", 4), ("MB", 3), ("G2b", 6), ("G3b", 5), ("X1", 2), ("G2a", 7), ("G2b", 7), ("X", 0),
+    ("MA", 4), ("G4", 5), ("MB", 4), ("X", 1), ("X1", 3), ("G3a", 6), ("G3a", 7), ("G3b", 6),
+    ("MA", 5), ("G3b", 7), ("MB", 5), ("G4", 6), ("X", 2), ("X1", 4), ("Z", 0), ("G4", 7),
+    ("MA", 6), ("MB", 6), ("MA", 7), ("MB", 7), ("X", 3), ("X", 4), ("F", 0), ("X1", 5),
+    ("X1", 6), ("Z", 1), ("Z", 2), ("X1", 7), ("Z", 3), ("X", 5), ("X", 6), ("X", 7), ("Z", 4),
+    ("Z", 5), ("Z", 6), ("Z", 7), ("F", 1), ("F", 2), ("F", 3), ("F", 4), ("F", 5), ("F", 6),
+    ("F", 7),
+)
 
 
 def swap_bits(tiles, tile_bit, lane_bit):
@@ -38,8 +54,8 @@
 def kernel(
     t_hbm, v_hbm, am_s, im_s, im_v, pairs_v, eocc_v, evir_v, evir_s,
     out,
-    tbuf, vbuf, vhi, vlo, pre_s, pre_r, slab, shi, slo, part, xr, zb, zr, post_s, post_r, occ, imf,
-    load_sem, pre_ss, pre_rs, g_ss, g_rs, c_ss, c_rs, x_ss, x_rs, z_ss, z_rs, o_ss, o_rs,
+    tbuf, vbuf, vhi, vlo, pre_s, pre_r, slab, terms, part, xa, xf, zb, zr, post_s, post_r, occ, imf,
+    load_sem, pre_ss, pre_rs, g_ss, g_rs, c_ss, c_rs, x_ss, xa_rs, xf_rs, z_ss, z_rs, o_ss, o_rs,
 ):
     row = lax.axis_index("row")
     col = lax.axis_index("col")
@@ -61,19 +77,26 @@
     dev_z = (row, col_of(y, flip))
     dev_core = (row, chip * 2 + 1 - core)
     dev_zlo = (row_z, col)
+    right, left, across = lax.rem(x + 1, 4), lax.rem(x + 3, 4), lax.rem(x + 2, 4)
+    dev_right = (zlo * 4 + right, col)
+    dev_left = (zlo * 4 + left, col)
     own_off = 64 * (y // 2)
     send_off = 64 - own_off
 
     barrier = pltpu.get_barrier_semaphore()
     peers = [(r, col_far) for r in range(8)]
     peers += [dev_up, dev_down, dev_z, dev_core]
-    peers += [(zlo * 4 + lax.rem(x + dx, 4), col) for dx in (1, 2, 3)]
+    peers += [dev_right, dev_left]
     peers += [(row_z, lax.rem(col + j, 16)) for j in range(16) if j != 8]
     for peer in peers:
         pl.semaphore_signal(barrier, inc=1, device_id=peer, device_id_type=MESH)
 
-    t_load = pltpu.make_async_copy(t_hbm, tbuf, load_sem.at[16])
-    t_load.start()
+    def t_load(offset, which):
+        rows = pl.ds(pl.multiple_of(offset, 8), 64)
+        return pltpu.make_async_copy(t_hbm.at[rows], tbuf.at[rows], load_sem.at[which])
+
+    t_load(send_off, 16).start()
+    t_load(own_off, 17).start()
 
     def v_load(block):
         rows = pl.ds(block * 128, 128)
@@ -93,12 +116,22 @@
 
     imf[...] = im_v[...].astype(F32)
 
-    ids = lax.broadcasted_iota(jnp.int32, (256, 200), 1)
-    first = jnp.sum(jnp.where(pairs_v[:, 0:1] == ids, eocc_v[...], 0.0), axis=1, keepdims=True)
-    second = jnp.sum(jnp.where(pairs_v[:, 1:2] == ids, eocc_v[...], 0.0), axis=1, keepdims=True)
-    occ[...] = jnp.broadcast_to(first + second, (256, 128))
-
-    t_load.wait()
+    ids = lax.broadcasted_iota(jnp.int32, (128, 128), 1)
+    for block in range(2):
+        rows = slice(block * 128, (block + 1) * 128)
+        total = []
+        for j in range(2):
+            picked = jnp.transpose(jnp.broadcast_to(pairs_v[j : j + 1, rows], (128, 128)))
+            total.append(
+                jnp.sum(jnp.where(picked == ids, eocc_v[:, 0:128], 0.0), axis=1, keepdims=True)
+                + jnp.sum(
+                    jnp.where(picked[:, 0:72] == ids[:, 0:72] + 128, eocc_v[:, 128:200], 0.0),
+                    axis=1, keepdims=True,
+                )
+            )
+        occ[rows, :] = jnp.broadcast_to(total[0] + total[1], (128, 128))
+
+    t_load(send_off, 16).wait()
 
     def masked_tile(offset, q, j):
         rows = pl.ds(pl.multiple_of(offset + q * ROWS, 8), ROWS)
@@ -119,13 +152,10 @@
                 pre_s.at[q, r], pre_r.at[q, row], pre_ss.at[q], pre_rs.at[q], (r, col_far)
             ).start()
 
-    pre_shuffle(0)
+    for q in range(ROUNDS):
+        pre_shuffle(q)
     pl.semaphore_wait(barrier, len(peers))
-    pre_send(0)
-    pre_shuffle(1)
-    pre_send(1)
-    for q in range(2, ROUNDS):
-        pre_shuffle(q)
+    t_load(own_off, 17).wait()
 
     def convert(block, _):
         v_load(block).wait()
@@ -138,18 +168,18 @@
             vlo[rows, lanes] = lo
         return 0
 
-    def slot(q, yy, zz, rows=None):
+    def slot(q, yy, zz, lanes=None):
         ref = slab.at[q, core, yy * 2 + zz]
-        return ref if rows is None else ref.at[rows]
-
-    LOWER, UPPER = pl.ds(0, HALF), pl.ds(HALF, HALF)
-
-    def push(q, kind, yy, zz, device, rows=None):
-        ref = slot(q, yy, zz, rows)
+        return ref if lanes is None else ref.at[:, lanes]
+
+    LOWER, UPPER = pl.ds(0, 1024), pl.ds(1024, 1024)
+
+    def push(q, kind, yy, zz, device, lanes=None):
+        ref = slot(q, yy, zz, lanes)
         remote(ref, ref, g_ss.at[q], g_rs.at[q, kind], device).start()
 
-    def arrived(q, kind, yy, zz, rows=None):
-        drain(slot(q, yy, zz, rows), g_rs.at[q, kind])
+    def arrived(q, kind, yy, zz, lanes=None):
+        drain(slot(q, yy, zz, lanes), g_rs.at[q, kind])
 
     def to_core(q, yy, zz):
         ref = slot(q, yy, zz)
@@ -162,73 +192,102 @@
             tiles = swap_bits(tiles, bit, bit + 4)
         for j in range(16):
             slab[q, core, chip, :, j * 128 : (j + 1) * 128] = masked_tile(own_off, q, j) + tiles[j]
-        push(q, 0, y, zhi, dev_z)
         push(q, 1, y, zhi, dev_up)
         push(q, 2, y, zhi, dev_down)
+        push(q, 0, y, zhi, dev_z)
         to_core(q, y, zhi)
 
-    def g2(q):
+    def g2a(q):
         arrived(q, 1, down, zhi)
         push(q, 3, down, zhi, dev_up, LOWER)
-        to_core(q, down, zhi)
         arrived(q, 2, up, zhi)
         push(q, 4, up, zhi, dev_down, UPPER)
+        if q in Y_FIRST:
+            push(q, 5, down, zhi, dev_z)
+            push(q, 6, up, zhi, dev_z)
+        to_core(q, down, zhi)
         to_core(q, up, zhi)
+
+    def g2b(q):
         arrived(q, 0, y, flip)
-        push(q, 5, y, flip, dev_up)
-        push(q, 6, y, flip, dev_down)
+        if q not in Y_FIRST:
+            push(q, 5, y, flip, dev_up)
+            push(q, 6, y, flip, dev_down)
         to_core(q, y, flip)
 
-    def g3(q):
+    def g3a(q):
         arrived(q, 3, opposite, zhi, LOWER)
         arrived(q, 4, opposite, zhi, UPPER)
+        if q in Y_FIRST:
+            push(q, 7, opposite, zhi, dev_z)
         to_core(q, opposite, zhi)
+
+    def g3b(q):
         arrived(q, 5, down, flip)
-        push(q, 7, down, flip, dev_up, LOWER)
+        if q not in Y_FIRST:
+            push(q, 7, down, flip, dev_up, LOWER)
+        arrived(q, 6, up, flip)
+        if q not in Y_FIRST:
+            push(q, 8, up, flip, dev_down, UPPER)
         to_core(q, down, flip)
-        arrived(q, 6, up, flip)
-        push(q, 8, up, flip, dev_down, UPPER)
         to_core(q, up, flip)
 
     def g4(q):
-        arrived(q, 7, opposite, flip, LOWER)
-        arrived(q, 8, opposite, flip, UPPER)
+        if q in Y_FIRST:
+            arrived(q, 7, opposite, flip)
+        else:
+            arrived(q, 7, opposite, flip, LOWER)
+            arrived(q, 8, opposite, flip, UPPER)
         to_core(q, opposite, flip)
 
-    def mm(q):
+    def tile(q, n):
+        lanes = slice(n * 512, (n + 1) * 512)
+        dot = functools.partial(jnp.dot, preferred_element_type=F32)
+        both = dot(terms[q % 2], vhi[:, lanes])
+        acc = (both[:128] + both[128:]) + dot(terms[q % 2, :128], vlo[:, lanes])
+        part[q, :, :, :, :, lanes] = acc.reshape(2, 2, 4, ROWS, 512)
+        onward, back = (dev_right, dev_left) if n == 0 else (dev_left, dev_right)
+        near = left if n == 0 else right
+        remote(
+            part.at[q, :, :, across, :, lanes], xa.at[q, n], x_ss.at[q], xa_rs.at[q, n], onward
+        ).start()
+        remote(
+            part.at[q, :, :, near, :, lanes], xf.at[q, n], x_ss.at[q], xf_rs.at[q], back
+        ).start()
+
+    def ma(q):
         drain(slab.at[q, 0], c_rs.at[q])
         for k in range(2):
-            for c in range(8):
-                rows = slice((k * 8 + c) * ROWS, (k * 8 + c + 1) * ROWS)
-                hi, lo = split(slab[q, k, c])
-                shi[rows, :] = hi
-                slo[rows, :] = lo
-
-        def tile(n, _):
-            lanes = pl.ds(pl.multiple_of(n * 256, 256), 256)
-            dot = functools.partial(jnp.dot, preferred_element_type=F32)
-            acc = dot(shi[...], vhi[:, lanes])
-            acc += dot(slo[...], vhi[:, lanes])
-            acc += dot(shi[...], vlo[:, lanes])
-            part[q, :, :, :, :, lanes] = acc.reshape(2, 2, 4, ROWS, 256)
-            return 0
-
-        lax.fori_loop(0, 4, tile, 0)
-        for dx in (1, 2, 3):
-            there = lax.rem(x + dx, 4)
-            remote(
-                part.at[q, :, :, there], xr.at[q, dx - 1], x_ss.at[q], x_rs.at[q],
-                (zlo * 4 + there, col),
-            ).start()
+            for c in range(0, 8, 2):
+                hi, lo = split(slab[q, k, c : c + 2].reshape(16, 2048))
+                at = (k * 8 + c) * ROWS
+                terms[q % 2, at : at + 16, :] = hi
+                terms[q % 2, 128 + at : 144 + at, :] = lo
+        tile(q, 0)
+
+    def mb(q):
+        tile(q, 1)
+
+    def x1(q):
+        for n in range(2):
+            lanes = slice(n * 512, (n + 1) * 512)
+            onward, near = (dev_right, right) if n == 0 else (dev_left, left)
+            drain(xa.at[q, n], xa_rs.at[q, n])
+            for k in range(2):
+                for z in range(2):
+                    xa[q, n, k, z] = xa[q, n, k, z] + part[q, k, z, near, :, lanes]
+            remote(xa.at[q, n], xf.at[q, 2 + n], x_ss.at[q], xf_rs.at[q], onward).start()
 
     def rx(q):
-        drain(xr.at[q], x_rs.at[q])
+        drain(xf.at[q], xf_rs.at[q])
         for side in (1, 0):
             z = lax.rem(zlo + side, 2)
             for k in range(2):
-                zb[q, side, k] = (
-                    (part[q, k, z, x] + xr[q, 0, k, z]) + (xr[q, 1, k, z] + xr[q, 2, k, z])
-                )
+                for n in range(2):
+                    lanes = slice(n * 512, (n + 1) * 512)
+                    zb[q, side, k, :, lanes] = (part[q, k, z, x, :, lanes] + xf[q, n, k, z]) + xf[
+                        q, 2 + n, k, z
+                    ]
             if side:
                 remote(zb.at[q, 1], zr.at[q], z_ss.at[q], z_rs.at[q], dev_zlo).start()
 
@@ -268,29 +327,22 @@
             for bl in range(8):
                 out[out_rows(k, 1 - zlo, q), bl * 128 : (bl + 1) * 128] = tiles[k * 8 + bl]
 
-    def when(stage, q):
-        if 0 <= q < ROUNDS:
-            stage(q)
-
-    for i in range(ROUNDS + 3):
-        when(g1, i)
-        if i + 2 < ROUNDS:
-            pre_send(i + 2)
-        when(rz, i - 3)
-        if i == 0:
-            lax.fori_loop(0, 16, convert, 0)
-        when(g4, i - 1)
-        when(g2, i)
-        when(mm, i - 1)
-        when(rx, i - 2)
-        when(g3, i)
-        when(fin, i - 3)
+    def convert_four(i):
+        lax.fori_loop(4 * i, 4 * i + 4, convert, 0)
+
+    stages = {
+        "P": pre_send, "C": convert_four, "G1": g1, "G2a": g2a, "G2b": g2b, "G3a": g3a,
+        "G3b": g3b, "G4": g4, "MA": ma, "MB": mb, "X1": x1, "X": rx, "Z": rz, "F": fin,
+    }
+    for stage, q in ORDER:
+        stages[stage](q)
 
     for q in range(ROUNDS):
         drain(pre_s.at[q], pre_ss.at[q])
         drain(slab.at[q, 0, pl.ds(0, 7)], g_ss.at[q])
         drain(slab.at[q, 0], c_ss.at[q])
-        drain(xr.at[q], x_ss.at[q])
+        drain(xf.at[q], x_ss.at[q])
+        drain(xa.at[q], x_ss.at[q])
         drain(zr.at[q], z_ss.at[q])
         drain(post_s.at[q], o_ss.at[q])
 
@@ -304,7 +356,7 @@
     eps_vir = eps_vir.reshape(1, 128)
     return pl.pallas_call(
         kernel,
-        out_shape=jax.ShapeDtypeStruct((256, 1024), F32),
+        out_shape=pltpu.VMEM((256, 1024), F32),
         in_specs=[hbm, hbm, smem, smem, vmem, vmem, vmem, vmem, smem],
         out_specs=vmem,
         scratch_shapes=[
@@ -315,21 +367,21 @@
             pltpu.VMEM((n, 8, 2, ROWS, 128), F32),
             pltpu.VMEM((n, 8, 2, ROWS, 128), F32),
             pltpu.VMEM((n, 2, 8, ROWS, 2048), F32),
-            pltpu.VMEM((16 * ROWS, 2048), BF16),
-            pltpu.VMEM((16 * ROWS, 2048), BF16),
+            pltpu.VMEM((2, 32 * ROWS, 2048), BF16),
             pltpu.VMEM((n, 2, 2, 4, ROWS, 1024), F32),
-            pltpu.VMEM((n, 3, 2, 2, ROWS, 1024), F32),
+            pltpu.VMEM((n, 2, 2, 2, ROWS, 512), F32),
+            pltpu.VMEM((n, 4, 2, 2, ROWS, 512), F32),
             pltpu.VMEM((n, 2, 2, ROWS, 1024), F32),
             pltpu.VMEM((n, 2, ROWS, 1024), F32),
             pltpu.VMEM((n, 16, ROWS, 128), F32),
             pltpu.VMEM((n, 16, ROWS, 128), F32),
             pltpu.VMEM((256, 128), F32),
             pltpu.VMEM((128, 128), F32),
-            dma((17,)),
+            dma((18,)),
             dma((n,)), dma((n,)),
             dma((n,)), dma((n, 9)),
             dma((n,)), dma((n,)),
-            dma((n,)), dma((n,)),
+            dma((n,)), dma((n, 2)), dma((n,)),
             dma((n,)), dma((n,)),
             dma((n,)), dma((n,)),
         ],
@@ -341,7 +393,7 @@
         ),
         name="ladder",
     )(
-        amplitudes, integrals, amp_mask, int_mask, int_mask, pairs,
+        amplitudes, integrals, amp_mask, int_mask, int_mask, pairs.T,
         eps_occ.reshape(1, 200), eps_vir, eps_vir,
     )
 

time: 113 us -> 86.7 us (0.77)
  Pallas kernels: 109 us -> 85.5 us
  local copies, waits for them, and re-layouts: 3.78 us -> 0.97 us
    pallas_call x1, Pallas kernels: 109 us -> 85.5 us  [on_device(): pl.pallas_call(kernel, out_shape=pltpu.VMEM((256, 1024), F32), in_specs=[...]
    unnamed x2 -> x1, local copies, waits for them, and re-layouts: 3.78 us -> 0.97 us
where the time goes in v2:
time: 86.7 us; the launch traced here: 86.5 us
  Pallas kernels  85.5 us (99%)
  local copies, waits for them, and re-layouts  0.97 us (1%)
    pallas_call x1, Pallas kernels, on_device(): pl.pallas_call(kernel, out_shape=pltpu.VMEM((256, 1024), F32), in_specs=[...  85.5 us

profile of v2, /device:TPU:1, one launch (start us, length us, event | category | flops | bytes accessed | tf_op | source)
XLA Modules:
  0.0 86.5 jit_solution(3916366635891528244)
XLA Ops:
  0.0 85.5 %ladder.1 = f32[256,1024]{1,0:T(8,128)S(1)} custom-call(f32[128,2048]{1,0:T(8,128)} %t_hbm.1, f32[2048,1024]{1,0:T(8,128)} %v_hbm.1, s32[16,128]{1,0:T(8,128)} %am_s.1, s32[128,128]{1,0:T(8,128)} %im_v.1, s32[128,128]{1,0:T(8,128)} %im_v.1, s32[2,256]{1,0:T(2,128)} %bitcast.3, f32[1,200]{1,0:T(1,128)} %bitcast.4, f32[1,128]{1,0:T(1,128)} %bitcast.5, ...), custom_call_target="tpu_custom_call" | custom-call | flops 12884901888 | bytes 10485760 | tf_op jit(solution)/shard_map/ladder/pallas_call | solution.py:357
  85.5 1.0 %copy.9 = f32[256,1024]{1,0:T(8,128)} copy(f32[256,1024]{1,0:T(8,128)S(1)} %ladder.1) | data formatting | bytes 2097152

commit v3 on v2

v3 whole, which is shorter than its diff:
```python
import functools

import jax
import jax.numpy as jnp
from jax import lax
from jax.experimental import pallas as pl
from jax.experimental.pallas import tpu as pltpu
from jax.sharding import PartitionSpec as P

MESH = pl.DeviceIdType.MESH
ROUNDS = 8
ROWS = 64 // ROUNDS
F32 = jnp.float32
BF16 = jnp.bfloat16
Y_FIRST = frozenset((0, 3, 5,))
EARLY = (6, 7,)
ORDER = (
    ("P", 0), ("P", 1), ("P", 2), ("P", 3), ("C", 0), ("C", 1), ("P", 4), ("G1", 0), ("G1", 1),
    ("G1", 2), ("C", 2), ("C", 3), ("G2a", 0), ("G1", 3), ("G2a", 1), ("G2a", 2), ("G2b", 0),
    ("G2b", 1), ("G3a", 0), ("G2b", 2), ("P", 5), ("G3a", 1), ("G2a", 3), ("MA", 0), ("G3b", 0),
    ("G3a", 2), ("G3b", 1), ("P", 6), ("MA", 1), ("G4", 0), ("G1", 4), ("G3b", 2), ("P", 7),
    ("MA", 2), ("G4", 1), ("MB", 0), ("G3a", 3), ("G2b", 3), ("X1A", 0), ("G1", 5), ("G2b", 4),
    ("MB", 1), ("G1", 6), ("G4", 2), ("G2a", 4), ("MA", 3), ("X1A", 1), ("X1B", 0), ("G3b", 3),
    ("G4", 3), ("G1", 7), ("G2a", 5), ("X1A", 2), ("XA", 0), ("MB", 2), ("G2a", 6), ("X1A", 3),
    ("G2b", 5), ("G3a", 4), ("G3b", 4), ("G2b", 6), ("MB", 3), ("XA", 1), ("XB", 0), ("X1B", 1),
    ("G3a", 5), ("MA", 4), ("X1B", 2), ("G4", 4), ("XA", 2), ("G3a", 6), ("G2b", 7), ("MA", 5),
    ("G3b", 5), ("G3b", 6), ("X1B", 3), ("G2a", 7), ("MB", 4), ("X1A", 4), ("XA", 3), ("ZA", 0),
    ("ZA", 1), ("XB", 1), ("G4", 5), ("MA", 6), ("G4", 6), ("G3b", 7), ("XB", 2), ("G3a", 7),
    ("X1A", 5), ("ZA", 2), ("MB", 5), ("X1B", 4), ("MB", 6), ("XB", 3), ("ZB", 0), ("G4", 7),
    ("XA", 4), ("MA", 7), ("X1B", 5), ("XA", 5), ("ZB", 1), ("ZA", 3), ("X1A", 6), ("MB", 7),
    ("XB", 4), ("ZA", 4), ("ZB", 2), ("ZB", 3), ("X1A", 7), ("ZA", 5), ("X1B", 6), ("XB", 5),
    ("XA", 6), ("X1B", 7), ("ZB", 4), ("XA", 7), ("F", 0), ("XB", 6), ("F", 1), ("F", 2),
    ("F", 3), ("ZA", 6), ("ZB", 5), ("XB", 7), ("F", 4), ("ZA", 7), ("F", 5), ("ZB", 6), ("F", 6),
    ("ZB", 7), ("F", 7),
)


def swap_bits(tiles, tile_bit, lane_bit):
    step = 1 << lane_bit
    lane = lax.broadcasted_iota(jnp.int32, tiles[0].shape, len(tiles[0].shape) - 1)
    upper = (lane & step) != 0
    result = list(tiles)
    for low in range(len(tiles)):
        if low >> tile_bit & 1:
            continue
        high = low | 1 << tile_bit
        a, b = tiles[low], tiles[high]
        result[low] = jnp.where(upper, pltpu.roll(b, step, 1), a)
        result[high] = jnp.where(upper, b, pltpu.roll(a, 128 - step, 1))
    return result


def split(value):
    hi = value.astype(BF16)
    return hi, (value - hi.astype(F32)).astype(BF16)


def kernel(
    t_hbm, v_hbm, am_s, im_s, im_v, pairs_v, eocc_v, evir_v, evir_s,
    out,
    tbuf, vbuf, vhi, vlo, pre_s, pre_r, slab, terms, part, xa, xf, zb, zr, post_s, post_r, twin_s, twin_r, occ, imf,
    load_sem, pre_ss, pre_rs, g_ss, g_rs, c_ss, c_rs, x_ss, xa_rs, xf_rs, z_ss, z_rs, o_ss, o_rs,
):
    row = lax.axis_index("row")
    col = lax.axis_index("col")
    zlo, x = row // 4, lax.rem(row, 4)
    y, zhi, core = col // 4, lax.rem(col // 2, 2), lax.rem(col, 2)
    chip = col // 2
    row_z = lax.rem(row + 4, 8)
    col_far = lax.rem(col + 8, 16)
    up = lax.rem(y + 1, 4)
    down = lax.rem(y + 3, 4)
    opposite = lax.rem(y + 2, 4)
    flip = 1 - zhi

    def col_of(yy, zz):
        return yy * 4 + zz * 2 + core

    dev_up = (row, col_of(up, zhi))
    dev_down = (row, col_of(down, zhi))
    dev_z = (row, col_of(y, flip))
    dev_core = (row, chip * 2 + 1 - core)
    dev_zlo = (row_z, col)
    right, left, across = lax.rem(x + 1, 4), lax.rem(x + 3, 4), lax.rem(x + 2, 4)
    dev_right = (zlo * 4 + right, col)
    dev_left = (zlo * 4 + left, col)
    own_off = 64 * (y // 2)
    send_off = 64 - own_off

    barrier = pltpu.get_barrier_semaphore()
    peers = [(r, col_far) for r in range(8)]
    peers += [(row, lax.rem(col + j, 16)) for j in range(1, 16)]
    peers += [dev_right, dev_left]
    peers += [(row_z, lax.rem(col + j, 16)) for j in range(16) if j != 8]
    for peer in peers:
        pl.semaphore_signal(barrier, inc=1, device_id=peer, device_id_type=MESH)

    def t_load(offset, count, which):
        rows = pl.ds(pl.multiple_of(offset, 8), count)
        return pltpu.make_async_copy(t_hbm.at[rows], tbuf.at[rows], load_sem.at[which])

    t_first = t_load(send_off, 2 * ROWS, 16)
    t_rest = t_load(send_off + 2 * ROWS, 64 - 2 * ROWS, 17)
    t_own = t_load(own_off, 64, 18)
    for load in (t_first, t_rest, t_own):
        load.start()

    def v_load(block):
        rows = pl.ds(block * 128, 128)
        return pltpu.make_async_copy(v_hbm.at[rows], vbuf.at[rows], load_sem.at[block])

    for block in range(16):
        v_load(block).start()

    def remote(src, dst, send_sem, recv_sem, device):
        return pltpu.make_async_remote_copy(
            src_ref=src, dst_ref=dst, send_sem=send_sem, recv_sem=recv_sem,
            device_id=device, device_id_type=MESH,
        )

    def drain(ref, sem):
        pltpu.make_async_copy(ref, ref, sem).wait()


    def masked_tile(offset, q, j):
        rows = pl.ds(pl.multiple_of(offset + q * ROWS, 8), ROWS)
        return tbuf[rows, j * 128 : (j + 1) * 128] * am_s[col, row * 16 + j].astype(F32)

    def pre_shuffle(q):
        tiles = [masked_tile(send_off, q, j) for j in range(16)]
        for bit in range(4):
            tiles = swap_bits(tiles, bit, bit)
        for bit in range(3):
            tiles = swap_bits(tiles, bit, bit + 4)
        for j in range(16):
            pre_s[q, j % 8, j // 8] = tiles[j]

    def pre_send(q):
        if q == 2:
            t_rest.wait()
        if q >= 2:
            pre_shuffle(q)
        for r in range(8):
            remote(
                pre_s.at[q, r], pre_r.at[q, row], pre_ss.at[q], pre_rs.at[q], (r, col_far)
            ).start()

    t_first.wait()
    pre_shuffle(0)
    pre_shuffle(1)
    pl.semaphore_wait(barrier, len(peers))

    def constants():
        imf[...] = im_v[...].astype(F32)

        ids = lax.broadcasted_iota(jnp.int32, (128, 128), 1)
        for block in range(2):
            rows = slice(block * 128, (block + 1) * 128)
            total = []
            for j in range(2):
                picked = jnp.transpose(jnp.broadcast_to(pairs_v[j : j + 1, rows], (128, 128)))
                total.append(
                    jnp.sum(jnp.where(picked == ids, eocc_v[:, 0:128], 0.0), axis=1, keepdims=True)
                    + jnp.sum(
                        jnp.where(picked[:, 0:72] == ids[:, 0:72] + 128, eocc_v[:, 128:200], 0.0),
                        axis=1, keepdims=True,
                    )
                )
            occ[rows, :] = jnp.broadcast_to(total[0] + total[1], (128, 128))

    def convert(block, _):
        v_load(block).wait()
        rows = pl.ds(pl.multiple_of(block * 128, 128), 128)
        for al in range(8):
            lanes = slice(al * 128, (al + 1) * 128)
            weight = im_s[row * 16 + block, col * 8 + al].astype(F32)
            hi, lo = split(vbuf[rows, lanes] * imf[...] * weight)
            vhi[rows, lanes] = hi
            vlo[rows, lanes] = lo
        return 0

    def slot(q, yy, zz, lanes=None):
        ref = slab.at[q, core, yy, zz]
        return ref if lanes is None else ref.at[:, lanes]

    LOWER, UPPER = pl.ds(0, 1024), pl.ds(1024, 1024)

    def push(q, kind, yy, zz, device, lanes=None):
        ref = slot(q, yy, zz, lanes)
        remote(ref, ref, g_ss.at[q], g_rs.at[q, kind], device).start()

    def arrived(q, kind, yy, zz, lanes=None):
        drain(slot(q, yy, zz, lanes), g_rs.at[q, kind])

    def to_core(q, yy, zz):
        ref = slot(q, yy, zz)
        half = 0 if zz is zhi else 1
        remote(ref, ref, c_ss.at[q], c_rs.at[q, half], dev_core).start()

    def g1(q):
        if q == 0:
            t_own.wait()
        drain(pre_r.at[q], pre_rs.at[q])
        tiles = [pre_r[q, j % 8, j // 8] for j in range(16)]
        for bit in range(3):
            tiles = swap_bits(tiles, bit, bit + 4)
        for j in range(16):
            slab[q, core, y, zhi, :, j * 128 : (j + 1) * 128] = masked_tile(own_off, q, j) + tiles[j]
        push(q, 1, y, zhi, dev_up)
        push(q, 2, y, zhi, dev_down)
        push(q, 0, y, zhi, dev_z)
        to_core(q, y, zhi)

    def g2a(q):
        arrived(q, 1, down, zhi)
        push(q, 3, down, zhi, dev_up, LOWER)
        arrived(q, 2, up, zhi)
        push(q, 4, up, zhi, dev_down, UPPER)
        if q in Y_FIRST:
            push(q, 5, down, zhi, dev_z)
            push(q, 6, up, zhi, dev_z)
        to_core(q, down, zhi)
        to_core(q, up, zhi)

    def g2b(q):
        arrived(q, 0, y, flip)
        if q not in Y_FIRST:
            push(q, 5, y, flip, dev_up)
            push(q, 6, y, flip, dev_down)
        to_core(q, y, flip)

    def g3a(q):
        arrived(q, 3, opposite, zhi, LOWER)
        arrived(q, 4, opposite, zhi, UPPER)
        if q in Y_FIRST:
            push(q, 7, opposite, zhi, dev_z)
        to_core(q, opposite, zhi)

    def g3b(q):
        arrived(q, 5, down, flip)
        if q not in Y_FIRST:
            push(q, 7, down, flip, dev_up, LOWER)
        arrived(q, 6, up, flip)
        if q not in Y_FIRST:
            push(q, 8, up, flip, dev_down, UPPER)
        to_core(q, down, flip)
        to_core(q, up, flip)

    def g4(q):
        if q in Y_FIRST:
            arrived(q, 7, opposite, flip)
        else:
            arrived(q, 7, opposite, flip, LOWER)
            arrived(q, 8, opposite, flip, UPPER)
        to_core(q, opposite, flip)

    parity = lax.rem(x, 2)

    def mm(q, plane, half):
        drain(slab.at[q, 0, pl.ds(0, 2)], c_rs.at[q, half])
        for k in range(2):
            for yy in range(0, 4, 2):
                value = jnp.concatenate([slab[q, k, yy, plane], slab[q, k, yy + 1, plane]], axis=0)
                hi, lo = split(value)
                at = (k * 4 + yy) * ROWS
                terms[half, at : at + 16, :] = hi
                terms[half, 64 + at : 80 + at, :] = lo
        for n in range(2):
            lanes = slice(n * 512, (n + 1) * 512)
            dot = functools.partial(jnp.dot, preferred_element_type=F32)
            both = dot(terms[half], vhi[:, lanes])
            acc = (both[:64] + both[64:]) + dot(terms[half, :64], vlo[:, lanes])
            part[q, plane, :, :, :, :, lanes] = acc.reshape(2, 2, 2, ROWS, 512)
            onward, back = (dev_right, dev_left) if n == 0 else (dev_left, dev_right)
            near = left if n == 0 else right

            @pl.when(parity == plane)
            def _():
                remote(
                    part.at[q, plane, :, :, across // 2, :, lanes], xa.at[q, n], x_ss.at[q],
                    xa_rs.at[q, n], onward,
                ).start()

            @pl.when(parity != plane)
            def _():
                remote(
                    part.at[q, plane, :, :, near // 2, :, lanes], xf.at[q, n], x_ss.at[q],
                    xf_rs.at[q], back,
                ).start()

    def join(q, plane):
        @pl.when(parity != plane)
        def _():
            for n in range(2):
                lanes = slice(n * 512, (n + 1) * 512)
                onward, near = (dev_right, right) if n == 0 else (dev_left, left)
                drain(xa.at[q, n], xa_rs.at[q, n])
                for k in range(2):
                    for z in range(2):
                        xa[q, n, k, z] = xa[q, n, k, z] + part[q, plane, k, z, near // 2, :, lanes]
                remote(xa.at[q, n], xf.at[q, 2 + n], x_ss.at[q], xf_rs.at[q], onward).start()

    def spread(tiles):
        for bit in range(3):
            tiles = swap_bits(tiles, bit, bit)
        for bit in range(3):
            tiles = swap_bits(tiles, bit, bit + 3)
        return swap_bits(tiles, 3, 6)

    def total(q, plane):
        @pl.when(parity == plane)
        def _():
            drain(xf.at[q], xf_rs.at[q])
            for side in (1, 0):
                z = lax.rem(zlo + side, 2)
                for k in range(2):
                    for n in range(2):
                        lanes = slice(n * 512, (n + 1) * 512)
                        zb[q, side, k, :, lanes] = (
                            part[q, plane, k, z, x // 2, :, lanes] + xf[q, n, k, z]
                        ) + xf[q, 2 + n, k, z]
                if side:
                    remote(zb.at[q, 1], zr.at[q], z_ss.at[q], z_rs.at[q], dev_zlo).start()
            if q in EARLY:
                e = EARLY.index(q)
                for side, there in ((0, row_z), (1, row)):
                    tiles = spread([
                        zb[q, side, k, :, al * 128 : (al + 1) * 128]
                        for k in range(2) for al in range(8)
                    ])
                    for c in range(16):
                        twin_s[e, side * 16 + c] = tiles[c]
                    for c in range(16):
                        copy = remote(
                            twin_s.at[e, side * 16 + c], twin_r.at[e, side * 16 + col],
                            o_ss.at[q], o_rs.at[q], (there, c),
                        )
                        if side:
                            pl.when(c != col)(copy.start)
                        else:
                            copy.start()
                twin_r[e, 16 + col] = twin_s[e, 16 + col]

    def out_rows(k, z, q):
        return pl.ds(pl.multiple_of(k * 128 + 64 * z + q * ROWS, 8), ROWS)

    def denominator(k, z, q, al):
        return (evir_s[0, col * 8 + al] + evir_v[...]) - occ[out_rows(k, z, q), :]

    def finish(q, plane):
        @pl.when(parity == plane)
        def _():
            drain(zr.at[q], z_rs.at[q])
            tiles = []
            for k in range(2):
                for al in range(8):
                    lanes = slice(al * 128, (al + 1) * 128)
                    value = zb[q, 0, k, :, lanes] + zr[q, k, :, lanes]
                    value = value / denominator(k, zlo, q, al)
                    out[out_rows(k, zlo, q), lanes] = value
                    tiles.append(value)
            if q not in EARLY:
                tiles = spread(tiles)
                for c in range(16):
                    post_s[q, c] = tiles[c]
                for c in range(16):
                    remote(
                        post_s.at[q, c], post_r.at[q, col], o_ss.at[q], o_rs.at[q], (row_z, c)
                    ).start()

    def fin(q):
        if q in EARLY:
            e = EARLY.index(q)
            drain(twin_r.at[e, pl.ds(0, 31)], o_rs.at[q])
            tiles = [twin_r[e, c] + twin_r[e, 16 + c] for c in range(16)]
        else:
            drain(post_r.at[q], o_rs.at[q])
            tiles = [post_r[q, c] for c in range(16)]
        for bit in range(3):
            tiles = swap_bits(tiles, bit, bit + 3)
        tiles = swap_bits(tiles, 3, 6)
        for k in range(2):
            for bl in range(8):
                value = tiles[k * 8 + bl]
                if q in EARLY:
                    value = value / denominator(k, 1 - zlo, q, bl)
                out[out_rows(k, 1 - zlo, q), bl * 128 : (bl + 1) * 128] = value

    def convert_four(i):
        if i == 0:
            constants()
        lax.fori_loop(4 * i, 4 * i + 4, convert, 0)

    stages = {
        "P": pre_send, "C": convert_four, "G1": g1, "G2a": g2a, "G2b": g2b, "G3a": g3a,
        "G3b": g3b, "G4": g4, "F": fin,
        "MA": lambda q: mm(q, zhi, 0), "MB": lambda q: mm(q, flip, 1),
        "X1A": lambda q: join(q, zhi), "X1B": lambda q: join(q, flip),
        "XA": lambda q: total(q, zhi), "XB": lambda q: total(q, flip),
        "ZA": lambda q: finish(q, zhi), "ZB": lambda q: finish(q, flip),
    }
    for stage, q in ORDER:
        stages[stage](q)

    for q in range(ROUNDS):
        drain(pre_s.at[q], pre_ss.at[q])
        drain(vbuf.at[pl.ds(0, 112)], g_ss.at[q])
        drain(slab.at[q, 0], c_ss.at[q])
        drain(vbuf.at[pl.ds(0, 96)], x_ss.at[q])
        drain(zr.at[q], z_ss.at[q])
        if q in EARLY:
            e = EARLY.index(q)
            drain(twin_s.at[e, pl.ds(0, 31)], o_ss.at[q])
        else:
            drain(post_s.at[q], o_ss.at[q])


def on_device(amplitudes, integrals, amp_mask, int_mask, pairs, eps_occ, eps_vir):
    vmem = pl.BlockSpec(memory_space=pltpu.VMEM)
    smem = pl.BlockSpec(memory_space=pltpu.SMEM)
    hbm = pl.BlockSpec(memory_space=pl.ANY)
    dma = pltpu.SemaphoreType.DMA
    n = ROUNDS
    eps_vir = eps_vir.reshape(1, 128)
    return pl.pallas_call(
        kernel,
        out_shape=pltpu.VMEM((256, 1024), F32),
        in_specs=[hbm, hbm, smem, smem, vmem, vmem, vmem, vmem, smem],
        out_specs=vmem,
        scratch_shapes=[
            pltpu.VMEM((128, 2048), F32),
            pltpu.VMEM((2048, 1024), F32),
            pltpu.VMEM((2048, 1024), BF16),
            pltpu.VMEM((2048, 1024), BF16),
            pltpu.VMEM((n, 8, 2, ROWS, 128), F32),
            pltpu.VMEM((n, 8, 2, ROWS, 128), F32),
            pltpu.VMEM((n, 2, 4, 2, ROWS, 2048), F32),
            pltpu.VMEM((2, 16 * ROWS, 2048), BF16),
            pltpu.VMEM((n, 2, 2, 2, 2, ROWS, 1024), F32),
            pltpu.VMEM((n, 2, 2, 2, ROWS, 512), F32),
            pltpu.VMEM((n, 4, 2, 2, ROWS, 512), F32),
            pltpu.VMEM((n, 2, 2, ROWS, 1024), F32),
            pltpu.VMEM((n, 2, ROWS, 1024), F32),
            pltpu.VMEM((n, 16, ROWS, 128), F32),
            pltpu.VMEM((n, 16, ROWS, 128), F32),
            pltpu.VMEM((max(1, len(EARLY)), 32, ROWS, 128), F32),
            pltpu.VMEM((max(1, len(EARLY)), 32, ROWS, 128), F32),
            pltpu.VMEM((256, 128), F32),
            pltpu.VMEM((128, 128), F32),
            dma((19,)),
            dma((n,)), dma((n,)),
            dma((n,)), dma((n, 9)),
            dma((n,)), dma((n, 2)),
            dma((n,)), dma((n, 2)), dma((n,)),
            dma((n,)), dma((n,)),
            dma((n,)), dma((n,)),
        ],
        compiler_params=pltpu.CompilerParams(
            collective_id=0, has_side_effects=True, vmem_limit_bytes=60 * 2**20
        ),
        cost_estimate=pl.CostEstimate(
            flops=3 * 2 * 1024 * 2048 * 1024, bytes_accessed=10 * 2**20, transcendentals=0
        ),
        name="ladder",
    )(
        amplitudes, integrals, amp_mask, int_mask, int_mask, pairs.T,
        eps_occ.reshape(1, 200), eps_vir, eps_vir,
    )


def solution(mesh):
    return jax.shard_map(
        on_device,
        mesh=mesh,
        in_specs=(P("col", "row"), P("row", "col"), P(), P(), P("row", None), P(), P()),
        out_specs=P("row", "col"),
        check_vma=False,
    )
```

time: 86.7 us -> 85.4 us (0.985)
  Pallas kernels: 85.5 us -> 84.2 us
    pallas_call x1, Pallas kernels: 85.5 us -> 84.2 us  [on_device(): pl.pallas_call(kernel, out_shape=pltpu.VMEM((256, 1024), F32), in_specs=[...]
where the time goes in v3:
time: 85.4 us; the launch traced here: 85.2 us
  Pallas kernels  84.2 us (99%)
  local copies, waits for them, and re-layouts  0.97 us (1%)
    pallas_call x1, Pallas kernels, on_device(): pl.pallas_call(kernel, out_shape=pltpu.VMEM((256, 1024), F32), in_specs=[...  84.2 us

profile of v3, /device:TPU:1, one launch (start us, length us, event | category | flops | bytes accessed | tf_op | source)
XLA Modules:
  0.0 85.2 jit_solution(14622856111213245215)
XLA Ops:
  0.0 84.2 %ladder.1 = f32[256,1024]{1,0:T(8,128)S(1)} custom-call(f32[128,2048]{1,0:T(8,128)} %t_hbm.1, f32[2048,1024]{1,0:T(8,128)} %v_hbm.1, s32[16,128]{1,0:T(8,128)} %am_s.1, s32[128,128]{1,0:T(8,128)} %im_v.1, s32[128,128]{1,0:T(8,128)} %im_v.1, s32[2,256]{1,0:T(2,128)} %bitcast.3, f32[1,200]{1,0:T(1,128)} %bitcast.4, f32[1,128]{1,0:T(1,128)} %bitcast.5, ...), custom_call_target="tpu_custom_call" | custom-call | flops 12884901888 | bytes 10485760 | tf_op jit(solution)/shard_map/ladder/pallas_call | solution.py:425
  84.2 1.0 %copy.9 = f32[256,1024]{1,0:T(8,128)} copy(f32[256,1024]{1,0:T(8,128)S(1)} %ladder.1) | data formatting | bytes 2097152

commit v4 on v3

--- a/solution.py
+++ b/solution.py
@@ -13,24 +13,24 @@
 F32 = jnp.float32
 BF16 = jnp.bfloat16
 Y_FIRST = frozenset((0, 3, 5,))
-EARLY = (6, 7,)
+EARLY = (5, 6, 7,)
 ORDER = (
-    ("P", 0), ("P", 1), ("P", 2), ("P", 3), ("C", 0), ("C", 1), ("P", 4), ("G1", 0), ("G1", 1),
-    ("G1", 2), ("C", 2), ("C", 3), ("G2a", 0), ("G1", 3), ("G2a", 1), ("G2a", 2), ("G2b", 0),
-    ("G2b", 1), ("G3a", 0), ("G2b", 2), ("P", 5), ("G3a", 1), ("G2a", 3), ("MA", 0), ("G3b", 0),
-    ("G3a", 2), ("G3b", 1), ("P", 6), ("MA", 1), ("G4", 0), ("G1", 4), ("G3b", 2), ("P", 7),
-    ("MA", 2), ("G4", 1), ("MB", 0), ("G3a", 3), ("G2b", 3), ("X1A", 0), ("G1", 5), ("G2b", 4),
-    ("MB", 1), ("G1", 6), ("G4", 2), ("G2a", 4), ("MA", 3), ("X1A", 1), ("X1B", 0), ("G3b", 3),
-    ("G4", 3), ("G1", 7), ("G2a", 5), ("X1A", 2), ("XA", 0), ("MB", 2), ("G2a", 6), ("X1A", 3),
-    ("G2b", 5), ("G3a", 4), ("G3b", 4), ("G2b", 6), ("MB", 3), ("XA", 1), ("XB", 0), ("X1B", 1),
-    ("G3a", 5), ("MA", 4), ("X1B", 2), ("G4", 4), ("XA", 2), ("G3a", 6), ("G2b", 7), ("MA", 5),
-    ("G3b", 5), ("G3b", 6), ("X1B", 3), ("G2a", 7), ("MB", 4), ("X1A", 4), ("XA", 3), ("ZA", 0),
-    ("ZA", 1), ("XB", 1), ("G4", 5), ("MA", 6), ("G4", 6), ("G3b", 7), ("XB", 2), ("G3a", 7),
-    ("X1A", 5), ("ZA", 2), ("MB", 5), ("X1B", 4), ("MB", 6), ("XB", 3), ("ZB", 0), ("G4", 7),
-    ("XA", 4), ("MA", 7), ("X1B", 5), ("XA", 5), ("ZB", 1), ("ZA", 3), ("X1A", 6), ("MB", 7),
-    ("XB", 4), ("ZA", 4), ("ZB", 2), ("ZB", 3), ("X1A", 7), ("ZA", 5), ("X1B", 6), ("XB", 5),
-    ("XA", 6), ("X1B", 7), ("ZB", 4), ("XA", 7), ("F", 0), ("XB", 6), ("F", 1), ("F", 2),
-    ("F", 3), ("ZA", 6), ("ZB", 5), ("XB", 7), ("F", 4), ("ZA", 7), ("F", 5), ("ZB", 6), ("F", 6),
+    ("P", 0), ("P", 1), ("P", 2), ("C", 0), ("C", 1), ("C", 2), ("P", 3), ("P", 4), ("G1", 0),
+    ("G1", 1), ("G1", 2), ("G1", 3), ("C", 3), ("G2a", 0), ("G2a", 1), ("G2b", 0), ("G2a", 2),
+    ("P", 5), ("G2b", 1), ("G2a", 3), ("G3a", 0), ("G2b", 2), ("G1", 4), ("G2b", 3), ("G3a", 1),
+    ("G3a", 2), ("P", 6), ("MA", 0), ("G3b", 0), ("MA", 1), ("G3b", 1), ("G3a", 3), ("MA", 2),
+    ("G3b", 2), ("G1", 5), ("X1A", 0), ("G4", 0), ("G3b", 3), ("P", 7), ("G2a", 4), ("MA", 3),
+    ("G2b", 4), ("X1A", 1), ("G4", 1), ("MB", 0), ("G1", 6), ("G4", 2), ("G4", 3), ("G2a", 5),
+    ("X1A", 2), ("MB", 1), ("MB", 2), ("G2b", 5), ("X1B", 0), ("G3a", 4), ("X1A", 3), ("XA", 0),
+    ("G3b", 4), ("G1", 7), ("MB", 3), ("G3a", 5), ("G2a", 6), ("G2b", 6), ("MA", 4), ("G4", 4),
+    ("X1B", 1), ("MA", 5), ("XB", 0), ("G3b", 5), ("G2b", 7), ("MB", 4), ("G3a", 6), ("X1A", 4),
+    ("G3b", 6), ("G2a", 7), ("XA", 1), ("XB", 1), ("X1B", 2), ("XA", 2), ("G4", 5), ("XA", 3),
+    ("X1B", 3), ("MA", 6), ("X1A", 5), ("G3b", 7), ("ZA", 0), ("ZA", 1), ("G4", 6), ("MB", 5),
+    ("G3a", 7), ("XB", 2), ("ZA", 2), ("ZB", 0), ("X1B", 4), ("XA", 4), ("MB", 6), ("XB", 3),
+    ("G4", 7), ("X1A", 6), ("XA", 5), ("MA", 7), ("X1B", 5), ("ZB", 1), ("XB", 4), ("ZB", 2),
+    ("MB", 7), ("ZA", 3), ("ZB", 3), ("F", 0), ("ZA", 4), ("X1B", 6), ("XA", 6), ("X1A", 7),
+    ("XB", 5), ("X1B", 7), ("ZB", 4), ("ZA", 5), ("XB", 6), ("F", 1), ("F", 2), ("XA", 7),
+    ("XB", 7), ("ZB", 5), ("ZA", 6), ("ZB", 6), ("F", 3), ("F", 4), ("F", 5), ("F", 6), ("ZA", 7),
     ("ZB", 7), ("F", 7),
 )
 

time: 85.4 us -> 83.9 us (0.982)
  Pallas kernels: 84.2 us -> 82.7 us
    pallas_call x1, Pallas kernels: 84.2 us -> 82.7 us  [on_device(): pl.pallas_call(kernel, out_shape=pltpu.VMEM((256, 1024), F32), in_specs=[...]
where the time goes in v4:
time: 83.9 us; the launch traced here: 83.7 us
  Pallas kernels  82.7 us (99%)
  local copies, waits for them, and re-layouts  0.97 us (1%)
    pallas_call x1, Pallas kernels, on_device(): pl.pallas_call(kernel, out_shape=pltpu.VMEM((256, 1024), F32), in_specs=[...  82.7 us

profile of v4, /device:TPU:1, one launch (start us, length us, event | category | flops | bytes accessed | tf_op | source)
XLA Modules:
  0.0 83.7 jit_solution(7822882568918560739)
XLA Ops:
  0.0 82.7 %ladder.1 = f32[256,1024]{1,0:T(8,128)S(1)} custom-call(f32[128,2048]{1,0:T(8,128)} %t_hbm.1, f32[2048,1024]{1,0:T(8,128)} %v_hbm.1, s32[16,128]{1,0:T(8,128)} %am_s.1, s32[128,128]{1,0:T(8,128)} %im_v.1, s32[128,128]{1,0:T(8,128)} %im_v.1, s32[2,256]{1,0:T(2,128)} %bitcast.3, f32[1,200]{1,0:T(1,128)} %bitcast.4, f32[1,128]{1,0:T(1,128)} %bitcast.5, ...), custom_call_target="tpu_custom_call" | custom-call | flops 12884901888 | bytes 10485760 | tf_op jit(solution)/shard_map/ladder/pallas_call | solution.py:425
  82.8 1.0 %copy.9 = f32[256,1024]{1,0:T(8,128)} copy(f32[256,1024]{1,0:T(8,128)S(1)} %ladder.1) | data formatting | bytes 2097152

commit v5 on v4

--- a/solution.py
+++ b/solution.py
@@ -87,6 +87,16 @@
     own_off = 64 * (y // 2)
     send_off = 64 - own_off
 
+    def t_load(offset, count, which):
+        rows = pl.ds(pl.multiple_of(offset, 8), count)
+        return pltpu.make_async_copy(t_hbm.at[rows], tbuf.at[rows], load_sem.at[which])
+
+    t_first = t_load(send_off, 2 * ROWS, 16)
+    t_rest = t_load(send_off + 2 * ROWS, 64 - 2 * ROWS, 17)
+    t_own = t_load(own_off, 64, 18)
+    for load in (t_first, t_rest, t_own):
+        load.start()
+
     barrier = pltpu.get_barrier_semaphore()
     peers = [(r, col_far) for r in range(8)]
     peers += [(row, lax.rem(col + j, 16)) for j in range(1, 16)]
@@ -94,16 +104,6 @@
     peers += [(row_z, lax.rem(col + j, 16)) for j in range(16) if j != 8]
     for peer in peers:
         pl.semaphore_signal(barrier, inc=1, device_id=peer, device_id_type=MESH)
-
-    def t_load(offset, count, which):
-        rows = pl.ds(pl.multiple_of(offset, 8), count)
-        return pltpu.make_async_copy(t_hbm.at[rows], tbuf.at[rows], load_sem.at[which])
-
-    t_first = t_load(send_off, 2 * ROWS, 16)
-    t_rest = t_load(send_off + 2 * ROWS, 64 - 2 * ROWS, 17)
-    t_own = t_load(own_off, 64, 18)
-    for load in (t_first, t_rest, t_own):
-        load.start()
 
     def v_load(block):
         rows = pl.ds(block * 128, 128)
@@ -138,7 +138,7 @@
     def pre_send(q):
         if q == 2:
             t_rest.wait()
-        if q >= 2:
+        if q >= 1:
             pre_shuffle(q)
         for r in range(8):
             remote(
@@ -147,7 +147,6 @@
 
     t_first.wait()
     pre_shuffle(0)
-    pre_shuffle(1)
     pl.semaphore_wait(barrier, len(peers))
 
     def constants():

time: 83.9 us -> 83.6 us (level)
  no operation moved by 1% of the time
where the time goes in v5:
time: 83.6 us; the launch traced here: 83.4 us
  Pallas kernels  82.4 us (99%)
  local copies, waits for them, and re-layouts  0.97 us (1%)
    pallas_call x1, Pallas kernels, on_device(): pl.pallas_call(kernel, out_shape=pltpu.VMEM((256, 1024), F32), in_specs=[...  82.4 us

profile of v5, /device:TPU:1, one launch (start us, length us, event | category | flops | bytes accessed | tf_op | source)
XLA Modules:
  0.0 83.4 jit_solution(2541838115107550995)
XLA Ops:
  0.0 82.4 %ladder.1 = f32[256,1024]{1,0:T(8,128)S(1)} custom-call(f32[128,2048]{1,0:T(8,128)} %t_hbm.1, f32[2048,1024]{1,0:T(8,128)} %v_hbm.1, s32[16,128]{1,0:T(8,128)} %am_s.1, s32[128,128]{1,0:T(8,128)} %im_v.1, s32[128,128]{1,0:T(8,128)} %im_v.1, s32[2,256]{1,0:T(2,128)} %bitcast.3, f32[1,200]{1,0:T(1,128)} %bitcast.4, f32[1,128]{1,0:T(1,128)} %bitcast.5, ...), custom_call_target="tpu_custom_call" | custom-call | flops 12884901888 | bytes 10485760 | tf_op jit(solution)/shard_map/ladder/pallas_call | solution.py:424
  82.4 1.0 %copy.9 = f32[256,1024]{1,0:T(8,128)} copy(f32[256,1024]{1,0:T(8,128)S(1)} %ladder.1) | data formatting | bytes 2097152
